TPU v7x, 512 devices: a whole 4x8x8 slice. The times are simulated.
512 devices in a mesh: dp: 32 (over y_lo, z, core), row: 4 (over y_hi), col: 4 (over x).
Axes of the slice: x: 4, y: 8 (y_hi: 4, y_lo: 2; y = y_hi * 2 + y_lo), z: 8, core: 2. Of those that a mesh axis runs over, the one named last changes fastest.
Arguments:
- heads_out: bfloat16 [8192, 6144], P(('dp', 'col'), 'row'), may hold values from -6 to 6
- residual: bfloat16 [8192, 6144], P('dp', 'col'), may hold values from -6 to 6
- master: float32 [6144, 6144], P(('row', 'dp'), 'col'), may hold values from -6 to 6
- moment_one: float32 [6144, 6144], P(('row', 'dp'), 'col'), may hold values from -4 to 4
- moment_two: float32 [6144, 6144], P(('row', 'dp'), 'col'), may hold values from 0.05 to 2
- out_grad: bfloat16 [8192, 6144], P('dp', 'col'), may hold values from -6 to 6
Outputs:
- stream_out: bfloat16 [8192, 6144], P('dp', 'col')
- heads_grad: bfloat16 [8192, 6144], P(('dp', 'col'), 'row')
- weight_grad: float32 [6144, 6144], P(('row', 'dp'), 'col')
- new_master: float32 [6144, 6144], P(('row', 'dp'), 'col')
- new_moment_one: float32 [6144, 6144], P(('row', 'dp'), 'col')
- new_moment_two: float32 [6144, 6144], P(('row', 'dp'), 'col')
All inputs are finite; a program needn't handle non-finite values.
Results may differ from a plain program's by a relative error of at most 0.009.
Values may be sent and summed in bfloat16 or wider, within the bound.
A program may use at most 64 MiB of HBM per device.

v0:
```python
import math
import jax
import jax.numpy as jnp
from jax import lax
from jax.sharding import PartitionSpec as P

HEADS = 48
HEAD_DIM = 128
beta_one = 0.9
beta_two = 0.95
learn_rate = 0.1
weight_decay = 0.1
epsilon = 1e-08


def filled_up(lines, count):
    spare = -len(lines) % count
    return jnp.pad(lines, [(0, spare)] + [(0, 0)] * (lines.ndim - 1))


def sum_by_parts(shard, axis):
    lines = shard.reshape(-1, *shard.shape[1:][-1:])
    padded = filled_up(lines, lax.axis_size(axis))
    own = lax.psum_scatter(padded, axis, scatter_dimension=0, tiled=True)
    whole = lax.all_gather(own, axis, axis=0, tiled=True)
    return whole[: len(lines)].reshape(shard.shape)


def in_blocks(shard, dim, count):
    before, after = (shard.shape[:dim], shard.shape[dim + 1 :])
    return jnp.moveaxis(shard.reshape(*before, count, -1, *after), dim, 0)


def sent_and_summed(shard, axis, dim):
    count = lax.axis_size(axis)
    tiles = lax.all_to_all(in_blocks(shard, dim, count), axis, 0, 0, tiled=True)
    return jnp.sum(tiles.astype(jnp.float32), axis=0)


def owner_grads(gathered, out_grad, fan_scale):
    tile_grad = (
        lax.dot_general(
            gathered, out_grad, (((0,), (0,)), ((), ())), preferred_element_type=jnp.float32
        )
        * fan_scale
    )
    owners = lax.axis_size("dp")
    stacked = tile_grad.astype(jnp.bfloat16).reshape(
        owners, tile_grad.shape[0] // owners, tile_grad.shape[1]
    )
    received = lax.all_to_all(stacked, "dp", split_axis=0, concat_axis=0, tiled=True)
    return jnp.sum(received.astype(jnp.float32), axis=0)


def shards(heads_out, residual, master, moment_one, moment_two, out_grad):
    fan_scale = 1.0 / math.sqrt(HEADS * HEAD_DIM)
    local_weight = master.astype(jnp.bfloat16)
    gathered = lax.all_gather(heads_out, "col", axis=0, tiled=True)
    weight_grad = None
    weight_tile = lax.all_gather(local_weight, "dp", axis=0, tiled=True)
    partial_sum = jnp.dot(gathered, weight_tile, preferred_element_type=jnp.float32) * fan_scale
    head_terms = (
        lax.dot_general(
            out_grad, weight_tile, (((1,), (1,)), ((), ())), preferred_element_type=jnp.float32
        )
        * fan_scale
    )
    mixed_sum = sum_by_parts(partial_sum.astype(jnp.bfloat16), "row").astype(jnp.float32)
    stream_out = (residual.astype(jnp.float32) + mixed_sum).astype(jnp.bfloat16)
    heads_grad = sent_and_summed(head_terms.astype(jnp.bfloat16), "col", 0).astype(jnp.bfloat16)
    weight_grad = owner_grads(gathered, out_grad, fan_scale)
    new_moment_one = beta_one * moment_one + (1.0 - beta_one) * weight_grad
    new_moment_two = beta_two * moment_two + (1.0 - beta_two) * weight_grad * weight_grad
    bias_one = 1.0 - beta_one**10
    bias_two = 1.0 - beta_two**10
    direction = new_moment_one / bias_one / (jnp.sqrt(new_moment_two / bias_two) + epsilon)
    new_master = master - learn_rate * (direction + weight_decay * master)
    return (stream_out, heads_grad, weight_grad, new_master, new_moment_one, new_moment_two)


def solution(mesh):
    return jax.shard_map(
        shards,
        mesh=mesh,
        in_specs=(
            P(("dp", "col"), "row"),
            P("dp", "col"),
            P(("row", "dp"), "col"),
            P(("row", "dp"), "col"),
            P(("row", "dp"), "col"),
            P("dp", "col"),
        ),
        out_specs=(
            P("dp", "col"),
            P(("dp", "col"), "row"),
            P(("row", "dp"), "col"),
            P(("row", "dp"), "col"),
            P(("row", "dp"), "col"),
            P(("row", "dp"), "col"),
        ),
        check_vma=False,
    )
```

profile of v0, /device:TPU:4, one launch (start us, length us, event | category | flops | bytes accessed | tf_op | source)
XLA Modules:
  0.0 276.4 jit_solution(10970078683171486864)
XLA Ops:
  7.2 0.0 copy-start
  7.2 0.0 all-gather.2.cloned.1.call-start
  7.2 17.5 %all_gather.9 = bf16[256,1536]{1,0:T(8,128)(2,1)S(1)} all-gather(bf16[64,1536]{1,0:T(8,128)(2,1)} %param.6), channel_id=1, replica_groups=mesh['dp'=32,'row'=4,'col'=4] {'col'}, dimensions={0}, use_global_device_ids=true | all-gather | bytes 983040 | tf_op jit(solution)/shard_map/all_gather | solution.py:58
  24.7 0.0 copy-done
  24.7 1.4 fusion
  26.1 113.2 %all_to_all.10 = bf16[32,48,1536]{2,1,0:T(8,128)(2,1)S(1)} all-to-all(bf16[32,48,1536]{2,1,0:T(8,128)(2,1)S(1)} %bitcast.8), channel_id=1, replica_groups=mesh['dp'=32,'row'=4,'col'=4] {'dp'}, dimensions={0} | all-to-all | bytes 9437184 | tf_op jit(solution)/shard_map/all_to_all | solution.py:51
  139.3 0.0 copy-start.3
  139.3 0.0 copy-start.4
  139.3 0.0 copy-start.5
  139.3 0.7 convert_reduce_fusion
  140.0 0.3 copy-done.3
  140.3 0.1 copy-done.4
  140.3 0.1 copy-done.5
  140.4 0.0 copy-start.1
  140.4 1.1 multiply_subtract_fusion
  141.6 0.0 all-gather.2.cloned.1.call-update
  141.6 0.0 reduce-scatter.2.cloned.1.call-start
  141.7 69.5 %all-gather.2.cloned.1.call-done = bf16[1536,1536]{1,0:T(8,128)(2,1)} async-done(((bf16[48,1536]{1,0:T(8,128)(2,1)}), bf16[1536,1536]{1,0:T(8,128)(2,1)}) %all-gather.2.cloned.1.call-update) | async-done | bytes 4718608 | tf_op jit(solution)/shard_map/all_gather | solution.py:60
  211.1 4.6 %fusion.1 = bf16[256,1536]{1,0:T(8,128)(2,1)} fusion(bf16[256,1536]{1,0:T(8,128)(2,1)S(1)} %all_gather.9, bf16[1536,1536]{1,0:T(8,128)(2,1)} %all-gather.2.cloned.1.call-done), kind=kOutput, calls=%fused_computation.5 | convolution fusion | flops 1208745984 | bytes 6291456 | tf_op jit(solution)/shard_map/dot_general | solution.py:61
  215.7 0.0 copy-done.1
  215.7 0.0 reduce-scatter.2.cloned.1.call-update
  215.8 0.0 copy-start.2
  215.8 3.8 %fusion.2 = bf16[256,1536]{1,0:T(8,128)(2,1)S(1)} fusion(bf16[256,1536]{1,0:T(8,128)(2,1)S(1)} %copy-done, bf16[1536,1536]{1,0:T(8,128)(2,1)} %all-gather.2.cloned.1.call-done), kind=kOutput, calls=%fused_computation.6 | convolution fusion | flops 1208745984 | bytes 6291456 | tf_op jit(solution)/shard_map/dot_general | solution.py:63
  219.6 14.6 %all_to_all.11 = bf16[4,64,1536]{2,1,0:T(8,128)(2,1)S(1)} all-to-all(bf16[4,64,1536]{2,1,0:T(8,128)(2,1)S(1)} %bitcast.9), channel_id=1, replica_groups=mesh['dp'=32,'row'=4,'col'=4] {'col'}, dimensions={0} | all-to-all | bytes 1572864 | tf_op jit(solution)/shard_map/all_to_all | solution.py:36
  234.2 0.8 reduce_sum.21
  235.0 13.4 %reduce-scatter.2.cloned.1.call-done = bf16[64,1536]{1,0:T(8,128)(2,1)} async-done(((bf16[256,1536]{1,0:T(8,128)(2,1)}), bf16[64,1536]{1,0:T(8,128)(2,1)}) %reduce-scatter.2.cloned.1.call-update) | async-done | bytes 196624 | tf_op jit(solution)/shard_map/reduce_scatter | solution.py:24
  248.4 20.1 %all_gather.11 = bf16[256,1536]{1,0:T(8,128)(2,1)S(1)} all-gather(bf16[64,1536]{1,0:T(8,128)(2,1)} %reduce-scatter.2.cloned.1.call-done), channel_id=1, replica_groups=mesh['dp'=32,'row'=4,'col'=4] {'row'}, dimensions={0}, use_global_device_ids=true | all-gather | bytes 983040 | tf_op jit(solution)/shard_map/all_gather | solution.py:25
  268.5 0.0 copy-done.2
  268.5 1.1 add_convert_fusion
Async XLA Ops:
  7.2 17.5 %copy-start = (bf16[256,1536]{1,0:T(8,128)(2,1)S(1)}, bf16[256,1536]{1,0:T(8,128)(2,1)}, u32[]{:S(2)}) copy-start(bf16[256,1536]{1,0:T(8,128)(2,1)} %param.11) | copy-start | bytes 2359300
  7.2 203.9 %all-gather.2.cloned.1.call-start = ((), (), s32[]{:S(2)}) async-start(), calls=%async_computation.3 | async-start | bytes 4866048 | tf_op jit(solution)/shard_map/all_gather | solution.py:60
  139.3 1.0 copy-start.3
  139.3 1.0 copy-start.4
  139.3 1.1 copy-start.5
  140.4 75.3 %copy-start.1 = (f32[48,1536]{1,0:T(8,128)}, f32[48,1536]{1,0:T(8,128)S(1)}, u32[]{:S(2)}) copy-start(f32[48,1536]{1,0:T(8,128)S(1)} %convert_reduce_fusion) | copy-start | bytes 884740
  141.6 106.7 %reduce-scatter.2.cloned.1.call-start = ((), (), s32[]{:S(2)}) async-start(), calls=%async_computation.4 | async-start | bytes 983040 | tf_op jit(solution)/shard_map/reduce_scatter | solution.py:24
  215.8 52.8 %copy-start.2 = (bf16[256,1536]{1,0:T(8,128)(2,1)S(1)}, bf16[256,1536]{1,0:T(8,128)(2,1)}, u32[]{:S(2)}) copy-start(bf16[256,1536]{1,0:T(8,128)(2,1)} %param.7) | copy-start | bytes 2359300
Sparse Core Ops, SparseCore 0:
  141.7 69.3 all-gather.1
  215.9 32.4 reduce-scatter.1
where the time goes:
time: 277 us; the launch traced here: 276 us
  blocking collectives  165 us (60%)
  waiting for transfers between devices  82.9 us (30%)
  between operations  14.1 us (5%)
  matrix products  9.84 us (4%)
  other arithmetic  3.7 us (1%)
    all_to_all x1, blocking collectives, owner_grads(): lax.all_to_all(stacked, 'dp', split_axis=0, concat_axis=0, tiled=True)  113 us
    all_gather x1, waiting for transfers between devices, shards(): weight_tile = lax.all_gather(local_weight, 'dp', axis=0, tiled=True)  69.5 us
    all_gather x1, blocking collectives, sum_by_parts(): whole = lax.all_gather(own, axis, axis=0, tiled=True)  20.1 us
    all_gather x1, blocking collectives, shards(): gathered = lax.all_gather(heads_out, 'col', axis=0, tiled=True)  17.5 us
    all_to_all x1, blocking collectives, sent_and_summed(): tiles = lax.all_to_all(in_blocks(shard, dim, count), axis, 0, 0, tiled=True)  14.6 us
    reduce_scatter x1, waiting for transfers between devices, sum_by_parts(): own = lax.psum_scatter(padded, axis, scatter_dimension=0, tiled=True)  13.4 us
  transfers between devices with their start and end apart: 2, of which 2 were waited for; matrix products, arithmetic and copies ran while one was open for 2% of the time, Pallas kernels for 0%

commit v1 on v0

--- a/solution.py
+++ b/solution.py
@@ -57,7 +57,9 @@
     local_weight = master.astype(jnp.bfloat16)
     gathered = lax.all_gather(heads_out, "col", axis=0, tiled=True)
     weight_grad = None
-    weight_tile = lax.all_gather(local_weight, "dp", axis=0, tiled=True)
+    weight_tile = jnp.concatenate(
+        lax.all_to_all(jnp.stack([local_weight] * lax.axis_size("dp")), "dp", 0, 0), axis=0
+    )
     partial_sum = jnp.dot(gathered, weight_tile, preferred_element_type=jnp.float32) * fan_scale
     head_terms = (
         lax.dot_general(

time: 277 us -> 319 us (1.15)
  blocking collectives: 165 us -> 279 us
  waiting for transfers between devices: 82.9 us -> 11.5 us
    all_to_all x0 -> x1, blocking collectives: none -> 111 us  [shards(): lax.all_to_all(jnp.stack([local_weight] * lax.axis_size('dp')), 'dp', 0, 0)]
    all_gather x1 -> x0, waiting for transfers between devices: 69.5 us -> none  [shards(): weight_tile = lax.all_gather(local_weight, 'dp', axis=0, tiled=True)]
  transfers between devices with their start and end apart: 2 -> 1, of which waited for: 2 -> 1; matrix products, arithmetic and copies ran while one was open for 2% -> 1% of each run, Pallas kernels for 0% -> 0%
where the time goes in v1:
time: 319 us; the launch traced here: 318 us
  blocking collectives  279 us (87%)
  between operations  14.1 us (4%)
  waiting for transfers between devices  11.5 us (4%)
  matrix products  7.52 us (2%)
  other arithmetic  3.61 us (1%)
    all_to_all x1, blocking collectives, owner_grads(): lax.all_to_all(stacked, 'dp', split_axis=0, concat_axis=0, tiled=True)  113 us
    all_to_all x1, blocking collectives, shards(): lax.all_to_all(jnp.stack([local_weight] * lax.axis_size('dp')), 'dp', 0, 0)  111 us
    all_gather x1, blocking collectives, sum_by_parts(): whole = lax.all_gather(own, axis, axis=0, tiled=True)  20.6 us
    all_gather x1, blocking collectives, shards(): gathered = lax.all_gather(heads_out, 'col', axis=0, tiled=True)  17.5 us
    all_to_all x1, blocking collectives, sent_and_summed(): tiles = lax.all_to_all(in_blocks(shard, dim, count), axis, 0, 0, tiled=True)  16 us
    reduce_scatter x1, waiting for transfers between devices, sum_by_parts(): own = lax.psum_scatter(padded, axis, scatter_dimension=0, tiled=True)  11.5 us
  transfers between devices with their start and end apart: 1, of which 1 were waited for; matrix products, arithmetic and copies ran while one was open for 1% of the time, Pallas kernels for 0%

profile of v1, /device:TPU:4, one launch (start us, length us, event | category | flops | bytes accessed | tf_op | source)
XLA Modules:
  0.0 318.4 jit_solution(16528245350887138770)
XLA Ops:
  7.2 0.0 copy-start
  7.2 0.0 reduce-scatter.2.cloned.1.call-start
  7.2 17.5 %all_gather.6 = bf16[256,1536]{1,0:T(8,128)(2,1)S(1)} all-gather(bf16[64,1536]{1,0:T(8,128)(2,1)} %param.6), channel_id=1, replica_groups=mesh['dp'=32,'row'=4,'col'=4] {'col'}, dimensions={0}, use_global_device_ids=true | all-gather | bytes 983040 | tf_op jit(solution)/shard_map/all_gather | solution.py:58
  24.7 0.0 copy-done
  24.7 1.4 fusion
  26.1 113.2 %all_to_all.15 = bf16[32,48,1536]{2,1,0:T(8,128)(2,1)S(1)} all-to-all(bf16[32,48,1536]{2,1,0:T(8,128)(2,1)S(1)} %bitcast.11), channel_id=1, replica_groups=mesh['dp'=32,'row'=4,'col'=4] {'dp'}, dimensions={0} | all-to-all | bytes 9437184 | tf_op jit(solution)/shard_map/all_to_all | solution.py:51
  139.3 0.0 copy-start.4
  139.3 0.0 copy-start.5
  139.3 0.0 copy-start.6
  139.3 0.7 convert_reduce_fusion
  140.0 0.3 copy-done.4
  140.3 0.1 copy-done.5
  140.4 0.1 copy-done.6
  140.4 0.0 copy-start.2
  140.5 1.1 multiply_subtract_fusion
  141.5 0.5 stack.2
  142.0 111.3 %all_to_all.16 = bf16[32,48,1536]{2,1,0:T(8,128)(2,1)S(1)} all-to-all(bf16[32,48,1536]{2,1,0:T(8,128)(2,1)S(1)} %stack.2), channel_id=1, replica_groups=mesh['dp'=32,'row'=4,'col'=4] {'dp'}, dimensions={0} | all-to-all | bytes 9437184 | tf_op jit(solution)/shard_map/all_to_all | solution.py:61
  253.4 0.0 copy-done.2
  253.4 0.0 copy-start.1
  253.4 2.1 copy-done.1
  255.5 2.3 fusion.1
  257.8 0.0 reduce-scatter.2.cloned.1.call-update
  257.8 0.0 copy-start.3
  257.8 3.8 %fusion.2 = bf16[256,1536]{1,0:T(8,128)(2,1)S(1)} fusion(bf16[256,1536]{1,0:T(8,128)(2,1)S(1)} %copy-done, bf16[1536,1536]{1,0:T(8,128)(2,1)} %bitcast.10), kind=kOutput, calls=%fused_computation.6 | convolution fusion | flops 1208745984 | bytes 6291456 | tf_op jit(solution)/shard_map/dot_general | solution.py:65
  261.6 16.0 %all_to_all.17 = bf16[4,64,1536]{2,1,0:T(8,128)(2,1)S(1)} all-to-all(bf16[4,64,1536]{2,1,0:T(8,128)(2,1)S(1)} %bitcast.12), channel_id=1, replica_groups=mesh['dp'=32,'row'=4,'col'=4] {'col'}, dimensions={0} | all-to-all | bytes 1572864 | tf_op jit(solution)/shard_map/all_to_all | solution.py:36
  277.6 0.8 reduce_sum.21
  278.4 11.5 %reduce-scatter.2.cloned.1.call-done = bf16[64,1536]{1,0:T(8,128)(2,1)} async-done(((bf16[256,1536]{1,0:T(8,128)(2,1)}), bf16[64,1536]{1,0:T(8,128)(2,1)}) %reduce-scatter.2.cloned.1.call-update) | async-done | bytes 196624 | tf_op jit(solution)/shard_map/reduce_scatter | solution.py:24
  289.9 20.6 %all_gather.7 = bf16[256,1536]{1,0:T(8,128)(2,1)S(1)} all-gather(bf16[64,1536]{1,0:T(8,128)(2,1)} %reduce-scatter.2.cloned.1.call-done), channel_id=1, replica_groups=mesh['dp'=32,'row'=4,'col'=4] {'row'}, dimensions={0}, use_global_device_ids=true | all-gather | bytes 983040 | tf_op jit(solution)/shard_map/all_gather | solution.py:25
  310.5 0.0 copy-done.3
  310.5 1.1 add_convert_fusion
Async XLA Ops:
  7.2 17.5 %copy-start = (bf16[256,1536]{1,0:T(8,128)(2,1)S(1)}, bf16[256,1536]{1,0:T(8,128)(2,1)}, u32[]{:S(2)}) copy-start(bf16[256,1536]{1,0:T(8,128)(2,1)} %param.11) | copy-start | bytes 2359300
  7.2 282.7 %reduce-scatter.2.cloned.1.call-start = ((), (), s32[]{:S(2)}) async-start(), calls=%async_computation.4 | async-start | bytes 983040 | tf_op jit(solution)/shard_map/reduce_scatter | solution.py:24
  139.3 1.0 copy-start.4
  139.3 1.0 copy-start.5
  139.3 1.1 copy-start.6
  140.4 112.9 %copy-start.2 = (f32[48,1536]{1,0:T(8,128)}, f32[48,1536]{1,0:T(8,128)S(1)}, u32[]{:S(2)}) copy-start(f32[48,1536]{1,0:T(8,128)S(1)} %convert_reduce_fusion) | copy-start | bytes 884740
  253.4 2.1 copy-start.1
  257.8 52.7 %copy-start.3 = (bf16[256,1536]{1,0:T(8,128)(2,1)S(1)}, bf16[256,1536]{1,0:T(8,128)(2,1)}, u32[]{:S(2)}) copy-start(bf16[256,1536]{1,0:T(8,128)(2,1)} %param.7) | copy-start | bytes 2359300
Sparse Core Ops, SparseCore 0:
  257.9 31.9 reduce-scatter.1
